TPU v7x, 32 devices: a whole 2x2x4 slice. The times are simulated.
32 devices in a mesh: head: 4 (over x, core), blk: 8 (over z, y).
Axes of the slice: x: 2, y: 2, z: 4, core: 2. Of those that a mesh axis runs over, the one named last changes fastest.
Arguments:
- queries: bfloat16 [8, 128, 6144], P('blk', 'head'), may hold values from -6 to 6
- keys: bfloat16 [8, 128, 6144], P('blk', 'head'), may hold values from -6 to 6
- values: bfloat16 [8, 128, 6144], P('blk', 'head'), may hold values from -6 to 6
- out_grad: bfloat16 [8, 128, 6144], P('blk', 'head'), may hold values from -96 to 96
- log_sum_exp: bfloat16 [48, 8, 128], P('head', 'blk'), may hold values from 7 to 9
- row_delta: bfloat16 [48, 8, 128], P('head', 'blk'), may hold values from -180 to 180
- assignment: int32 [8], replicated, may hold values from 0 to 7, as said below
- block_mask: int32 [16, 16], replicated, may hold values from 0 to 2, as said below
Outputs:
- query_grad: bfloat16 [8, 128, 6144], P('blk', 'head')
- key_grad: bfloat16 [8, 128, 6144], P('blk', 'head')
- value_grad: bfloat16 [8, 128, 6144], P('blk', 'head')
Inputs may be any that keep to these rules, and one draw needn't show every extreme that they name: A permutation of the pair indices; the slot d holds the blocks assignment[d] and 15 - assignment[d]. `block_mask`: 2 on the diagonal; 1 where the key block comes earlier than the query block and the slots holding the two blocks lie at most 2 apart around the cyclic order of slots; 0 elsewhere.
All inputs are finite; a program needn't handle non-finite values.
Results may differ from a plain program's by a relative error of at most 0.008.
Values may be sent and summed in bfloat16 or wider, within the bound.
A program may use at most 64 MiB of HBM per device.

v0:
```python
import jax
import jax.numpy as jnp
from jax import lax
from jax.sharding import PartitionSpec as P

HD = 128


def from_behind(value, axis, steps):
    count = lax.axis_size(axis)
    pairs = [(source, (source + steps) % count) for source in range(count)]
    return lax.ppermute(value, axis, pairs)


def pair_terms(query_pack, key_pack, allowed):
    query_rows, grad_rows, lse_rows, delta_rows = query_pack
    key_rows, value_rows = key_pack
    scaling = HD ** (-0.5)
    row_count = query_rows.shape[0]
    head_count = lse_rows.shape[0]
    q_three = query_rows.reshape(row_count, head_count, HD)
    g_three = grad_rows.reshape(row_count, head_count, HD)
    k_three = key_rows.reshape(row_count, head_count, HD)
    v_three = value_rows.reshape(row_count, head_count, HD)
    scores = (
        jnp.einsum("qhd,khd->hqk", q_three, k_three, preferred_element_type=jnp.float32) * scaling
    )
    probabilities = jnp.where(
        allowed[None], jnp.exp(scores - lse_rows.astype(jnp.float32)[:, :, None]), 0.0
    )
    prob_bf = probabilities.astype(jnp.bfloat16)
    dprobs = jnp.einsum("qhd,khd->hqk", g_three, v_three, preferred_element_type=jnp.float32)
    dscores = (probabilities * (dprobs - delta_rows.astype(jnp.float32)[:, :, None])).astype(
        jnp.bfloat16
    )
    dv_part = jnp.einsum("hqk,qhd->khd", prob_bf, g_three, preferred_element_type=jnp.float32)
    dk_part = scaling * jnp.einsum(
        "hqk,qhd->khd", dscores, q_three, preferred_element_type=jnp.float32
    )
    dq_part = scaling * jnp.einsum(
        "hqk,khd->qhd", dscores, k_three, preferred_element_type=jnp.float32
    )
    width = head_count * HD
    return (
        dq_part.reshape(row_count, width).astype(jnp.bfloat16),
        dk_part.reshape(row_count, width).astype(jnp.bfloat16),
        dv_part.reshape(row_count, width).astype(jnp.bfloat16),
    )


def local(queries, keys, values, out_grad, log_sum_exp, row_delta, assignment, block_mask):
    query_rows, key_rows, value_rows, grad_rows = (
        lax.all_to_all(queries, "head", split_axis=2, concat_axis=1, tiled=True),
        lax.all_to_all(keys, "head", split_axis=2, concat_axis=1, tiled=True),
        lax.all_to_all(values, "head", split_axis=2, concat_axis=1, tiled=True),
        lax.all_to_all(out_grad, "head", split_axis=2, concat_axis=1, tiled=True),
    )
    row_count = query_rows.shape[1]
    half_rows = row_count // 2
    query_rows = query_rows[0]
    key_rows = key_rows[0]
    value_rows = value_rows[0]
    grad_rows = grad_rows[0]
    lse_rows = log_sum_exp[:, 0, :]
    delta_rows = row_delta[:, 0, :]
    my_index = lax.axis_index("blk")
    slot_count = lax.axis_size("blk")
    cycle_steps = min(4, slot_count // 4)
    block_total = 2 * slot_count
    row_ids = jnp.arange(row_count, dtype=jnp.int32)
    low_rows = row_ids < half_rows
    row_offsets = row_ids % half_rows

    def allowed_for(query_slot, key_slot):
        q_low = assignment[jnp.mod(query_slot, slot_count)]
        k_low = assignment[jnp.mod(key_slot, slot_count)]
        q_high = block_total - 1 - q_low
        k_high = block_total - 1 - k_low
        upper_left = block_mask[q_low, k_low]
        upper_right = block_mask[q_low, k_high]
        lower_left = block_mask[q_high, k_low]
        lower_right = block_mask[q_high, k_high]
        upper = jnp.where(low_rows[None, :], upper_left, upper_right)
        lower = jnp.where(low_rows[None, :], lower_left, lower_right)
        table = jnp.where(low_rows[:, None], upper, lower)
        return (table == 1) | (table == 2) & (row_offsets[:, None] >= row_offsets[None, :])

    query_pack = (query_rows, grad_rows, lse_rows, delta_rows)
    key_pack = (key_rows, value_rows)
    dq_self, dk_self, dv_self = pair_terms(query_pack, key_pack, allowed_for(my_index, my_index))
    dq_total = dq_self.astype(jnp.float32)
    dk_total = dk_self.astype(jnp.float32)
    dv_total = dv_self.astype(jnp.float32)
    from_below = key_pack
    from_above = key_pack
    for step in range(1, cycle_steps + 1):
        from_below = from_behind((from_below[0], from_below[1]), "blk", 1)
        from_above = from_behind((from_above[0], from_above[1]), "blk", -1)
        dq_low, dk_low, dv_low = pair_terms(
            query_pack, from_below, allowed_for(my_index, my_index - step)
        )
        dq_high, dk_high, dv_high = pair_terms(
            query_pack, from_above, allowed_for(my_index, my_index + step)
        )
        dq_total = dq_total + dq_low.astype(jnp.float32) + dq_high.astype(jnp.float32)
        back_low = from_behind((dk_low, dv_low), "blk", -step)
        back_high = from_behind((dk_high, dv_high), "blk", step)
        dk_total = dk_total + back_low[0].astype(jnp.float32) + back_high[0].astype(jnp.float32)
        dv_total = dv_total + back_low[1].astype(jnp.float32) + back_high[1].astype(jnp.float32)
    query_grad = dq_total.astype(jnp.bfloat16)[None]
    key_grad = dk_total.astype(jnp.bfloat16)[None]
    value_grad = dv_total.astype(jnp.bfloat16)[None]
    return (
        lax.all_to_all(query_grad, "head", split_axis=1, concat_axis=2, tiled=True),
        lax.all_to_all(key_grad, "head", split_axis=1, concat_axis=2, tiled=True),
        lax.all_to_all(value_grad, "head", split_axis=1, concat_axis=2, tiled=True),
    )


def solution(mesh):
    placed = (
        P("blk", "head", None),
        P("blk", "head", None),
        P("blk", "head", None),
        P("blk", "head", None),
        P("head", "blk", None),
        P("head", "blk", None),
        P(),
        P(),
    )
    return jax.shard_map(
        local,
        mesh=mesh,
        in_specs=placed,
        out_specs=(P("blk", "head", None), P("blk", "head", None), P("blk", "head", None)),
        check_vma=False,
    )
```

profile of v0, /device:TPU:0, one launch (start us, length us, event | category | flops | bytes accessed | tf_op | source)
XLA Modules:
  0.0 431.4 jit_solution(11832265723801058477)
XLA Ops:
  0.6 6.1 %copy.249 = bf16[1,32,6144]{1,0,2:T(2,128)(2,1)S(1)} copy(bf16[1,32,6144]{2,1,0:T(8,128)(2,1)} %param.8) | data formatting | bytes 786432 | tf_op args[0]
  7.3 34.5 %reduce = bf16[6144,32]{1,0:T(8,128)(2,1)} reduce(bf16[6144,1,32]{2,1,0:T(2,128)(2,1)S(1)} %bitcast.173, bf16[]{:T(256)} %broadcast.496), dimensions={1}, to_apply=%bitcast.113.reduce_sub_computation | reduce | bytes 786434
  41.8 3.3 reshape.610
  45.1 4.4 %all-to-all-start = ((bf16[4,2,24576]{2,1,0:T(2,128)(2,1)}), bf16[4,2,24576]{2,1,0:T(2,128)(2,1)S(1)}, u32[]{:S(2)}, u32[]{:S(2)}) async-start(bf16[4,2,24576]{2,1,0:T(2,128)(2,1)} %reshape.610), calls=%async_computation | async-start | bytes 786432 | tf_op jit(solution)/shard_map/all_to_all | solution.py:53
  63.1 6.1 %copy.252 = bf16[1,32,6144]{1,0,2:T(2,128)(2,1)S(1)} copy(bf16[1,32,6144]{2,1,0:T(8,128)(2,1)} %param.9) | data formatting | bytes 786432 | tf_op args[1]
  69.2 34.5 %reduce.1 = bf16[6144,32]{1,0:T(8,128)(2,1)} reduce(bf16[6144,1,32]{2,1,0:T(2,128)(2,1)S(1)} %bitcast.178, bf16[]{:T(256)} %broadcast.496), dimensions={1}, to_apply=%bitcast.115.reduce_sub_computation | reduce | bytes 786434
  103.6 3.3 reshape.612
  106.9 6.1 %copy.257 = bf16[1,32,6144]{1,0,2:T(2,128)(2,1)S(1)} copy(bf16[1,32,6144]{2,1,0:T(8,128)(2,1)} %param.11) | data formatting | bytes 786432 | tf_op args[3]
  113.1 34.9 %reduce.2 = bf16[6144,32]{1,0:T(8,128)(2,1)} reduce(bf16[6144,1,32]{2,1,0:T(2,128)(2,1)S(1)} %bitcast.179, bf16[]{:T(256)} %broadcast.496), dimensions={1}, to_apply=%bitcast.117.reduce_sub_computation | reduce | bytes 786434
  147.9 3.3 reshape.614
  151.2 6.1 %copy.260 = bf16[1,32,6144]{1,0,2:T(2,128)(2,1)S(1)} copy(bf16[1,32,6144]{2,1,0:T(8,128)(2,1)} %param.10) | data formatting | bytes 786432 | tf_op args[2]
  157.4 34.5 %reduce.3 = bf16[6144,32]{1,0:T(8,128)(2,1)} reduce(bf16[6144,1,32]{2,1,0:T(2,128)(2,1)S(1)} %bitcast.180, bf16[]{:T(256)} %broadcast.496), dimensions={1}, to_apply=%bitcast.119.reduce_sub_computation | reduce | bytes 786434
  191.8 3.4 reshape.616
  199.3 1.3 and_select_fusion
  200.6 2.5 fusion.70
  203.1 2.4 fusion.72
  205.5 2.5 fusion.74
  208.0 3.5 all-to-all-start.1
  211.5 2.4 fusion.76
  213.9 5.0 %all-to-all-done.1 = bf16[4,2,24576]{2,1,0:T(2,128)(2,1)S(1)} async-done(((bf16[4,2,24576]{2,1,0:T(2,128)(2,1)}), bf16[4,2,24576]{2,1,0:T(2,128)(2,1)S(1)}, u32[]{:S(2)}, u32[]{:S(2)}) %all-to-all-start.1) | async-done | bytes 393248 | tf_op jit(solution)/shard_map/all_to_all | solution.py:54
  218.9 3.5 all-to-all-start.3
  222.4 7.4 %all-to-all-done.3 = bf16[4,2,24576]{2,1,0:T(2,128)(2,1)S(1)} async-done(((bf16[4,2,24576]{2,1,0:T(2,128)(2,1)}), bf16[4,2,24576]{2,1,0:T(2,128)(2,1)S(1)}, u32[]{:S(2)}, u32[]{:S(2)}) %all-to-all-start.3) | async-done | bytes 393248 | tf_op jit(solution)/shard_map/all_to_all | solution.py:55
  229.8 4.1 all-to-all-start.2
  233.9 1.3 fusion.78
  236.0 2.8 reshape.613
  238.8 4.7 %copy.253 = bf16[1,32,6144]{2,1,0:T(8,128)(2,1)} copy(bf16[1,32,6144]{1,0,2:T(2,128)(2,1)S(1)} %bitcast.174) | data formatting | bytes 786432 | tf_op jit(solution)/shard_map/all_to_all | solution.py:54
  243.6 1.3 all_to_all.87
  245.7 2.1 reshape_squeeze.9
  247.8 5.2 %collective-permute-start.2 = (bf16[128,1536]{1,0:T(8,128)(2,1)}, bf16[128,1536]{1,0:T(8,128)(2,1)}, u32[]{:S(2)}, u32[]{:S(2)}) collective-permute-start(bf16[128,1536]{1,0:T(8,128)(2,1)} %bitcast.16), channel_id=1, source_target_pairs={{0,7},{1,0},{2,1},{3,2},{4,3},{5,4},{6,5},{7,6},{8,15},{9,8},{10,9... | collective-permute-start | bytes 1179656 | tf_op jit(solution)/shard_map/ppermute | solution.py:12
  253.0 2.8 reshape.617
  255.8 4.7 %copy.261 = bf16[1,32,6144]{2,1,0:T(8,128)(2,1)} copy(bf16[1,32,6144]{1,0,2:T(2,128)(2,1)S(1)} %bitcast.175) | data formatting | bytes 786432 | tf_op jit(solution)/shard_map/all_to_all | solution.py:55
  260.6 1.3 all_to_all.93
  262.7 2.1 reshape_squeeze.11
  264.8 4.7 %collective-permute-start.3 = (bf16[128,1536]{1,0:T(8,128)(2,1)}, bf16[128,1536]{1,0:T(8,128)(2,1)}, u32[]{:S(2)}, u32[]{:S(2)}) collective-permute-start(bf16[128,1536]{1,0:T(8,128)(2,1)} %bitcast.18), channel_id=1, source_target_pairs={{0,7},{1,0},{2,1},{3,2},{4,3},{5,4},{6,5},{7,6},{8,15},{9,8},{10,9... | collective-permute-start | bytes 1179656 | tf_op jit(solution)/shard_map/ppermute | solution.py:12
  269.5 1.4 reshape.611
  270.9 3.0 copy.250
  275.0 2.8 reshape.615
  277.8 4.7 %copy.258 = bf16[1,32,6144]{2,1,0:T(8,128)(2,1)} copy(bf16[1,32,6144]{1,0,2:T(2,128)(2,1)S(1)} %bitcast.177) | data formatting | bytes 786432 | tf_op jit(solution)/shard_map/all_to_all | solution.py:56
  282.6 1.3 all_to_all.90
  285.8 1.5 fusion.24
  294.1 1.3 fusion.32
  298.6 1.9 copy.272
  300.5 1.4 fusion.23
  303.1 1.9 copy.305
  305.1 4.7 %collective-permute-start.8 = (bf16[128,1536]{0,1:T(8,128)(2,1)}, bf16[128,1536]{0,1:T(8,128)(2,1)}, u32[]{:S(2)}, u32[]{:S(2)}) collective-permute-start(bf16[128,1536]{0,1:T(8,128)(2,1)} %bitcast.213), channel_id=1, source_target_pairs={{0,7},{1,0},{2,1},{3,2},{4,3},{5,4},{6,5},{7,6},{8,15},{9,8},{10,9... | collective-permute-start | bytes 1179656 | tf_op jit(solution)/shard_map/ppermute | solution.py:12
  310.7 4.7 %collective-permute-start.6 = (bf16[128,1536]{1,0:T(8,128)(2,1)}, bf16[128,1536]{1,0:T(8,128)(2,1)S(1)}, u32[]{:S(2)}, u32[]{:S(2)}) collective-permute-start(bf16[128,1536]{1,0:T(8,128)(2,1)} %collective-permute-done.2), channel_id=1, source_target_pairs={{0,7},{1,0},{2,1},{3,2},{4,3},{5,4},{6,5},{7,6},{8,15},{9,8},{10,9... | collective-permute-start | bytes 1179656 | tf_op jit(solution)/shard_map/ppermute | solution.py:12
  315.5 2.4 fusion.30
  319.1 16.7 %collective-permute-done.6 = bf16[128,1536]{1,0:T(8,128)(2,1)S(1)} collective-permute-done((bf16[128,1536]{1,0:T(8,128)(2,1)}, bf16[128,1536]{1,0:T(8,128)(2,1)S(1)}, u32[]{:S(2)}, u32[]{:S(2)}) %collective-permute-start.6) | collective-permute-done | bytes 393248 | tf_op jit(solution)/shard_map/ppermute | solution.py:12
  336.5 16.1 %collective-permute-done.7 = bf16[128,1536]{1,0:T(8,128)(2,1)S(1)} collective-permute-done((bf16[128,1536]{1,0:T(8,128)(2,1)}, bf16[128,1536]{1,0:T(8,128)(2,1)S(1)}, u32[]{:S(2)}, u32[]{:S(2)}) %collective-permute-start.7) | collective-permute-done | bytes 393248 | tf_op jit(solution)/shard_map/ppermute | solution.py:12
  353.3 1.3 fusion.39
  356.6 11.1 %collective-permute-done.5 = bf16[128,1536]{1,0:T(8,128)(2,1)} collective-permute-done((bf16[128,1536]{1,0:T(8,128)(2,1)}, bf16[128,1536]{1,0:T(8,128)(2,1)}, u32[]{:S(2)}, u32[]{:S(2)}) %collective-permute-start.5) | collective-permute-done | bytes 393248 | tf_op jit(solution)/shard_map/ppermute | solution.py:12
  370.7 1.8 fusion.52
  373.7 3.0 reduce.4
  377.8 6.9 %all-to-all-start.4 = ((bf16[4,2,24576]{2,1,0:T(2,128)(2,1)}), bf16[4,2,24576]{2,1,0:T(2,128)(2,1)S(1)}, u32[]{:S(2)}, u32[]{:S(2)}) async-start(bf16[4,2,24576]{2,1,0:T(2,128)(2,1)} %reshape.618), calls=%async_computation.4 | async-start | bytes 786432 | tf_op jit(solution)/shard_map/all_to_all | solution.py:114
  386.3 4.0 collective-permute-start.14
  390.3 1.6 fusion.56
  392.7 3.0 reduce.5
  396.7 3.5 all-to-all-start.5
  400.2 4.8 %collective-permute-done.15 = bf16[128,1536]{1,0:T(8,128)(2,1)} collective-permute-done((bf16[128,1536]{1,0:T(8,128)(2,1)}, bf16[128,1536]{1,0:T(8,128)(2,1)}, u32[]{:S(2)}, u32[]{:S(2)}) %collective-permute-start.15) | collective-permute-done | bytes 393248 | tf_op jit(solution)/shard_map/ppermute | solution.py:12
  404.9 7.7 %collective-permute-done.14 = bf16[128,1536]{1,0:T(8,128)(2,1)} collective-permute-done((bf16[128,1536]{1,0:T(8,128)(2,1)S(1)}, bf16[128,1536]{1,0:T(8,128)(2,1)}, u32[]{:S(2)}, u32[]{:S(2)}) %collective-permute-start.14) | collective-permute-done | bytes 393248 | tf_op jit(solution)/shard_map/ppermute | solution.py:12
  412.6 1.6 fusion.57
  414.8 3.0 reduce.6
  418.8 3.5 all-to-all-start.6
  424.8 4.9 %all-to-all-done.6 = bf16[4,2,24576]{2,1,0:T(2,128)(2,1)S(1)} async-done(((bf16[4,2,24576]{2,1,0:T(2,128)(2,1)}), bf16[4,2,24576]{2,1,0:T(2,128)(2,1)S(1)}, u32[]{:S(2)}, u32[]{:S(2)}) %all-to-all-start.6) | async-done | bytes 393248 | tf_op jit(solution)/shard_map/all_to_all | solution.py:116
  (122 shorter events, 37.8 us)
Async XLA Ops:
  7.3 42.3 %copy-start.11 = (s32[8]{0:T(128)S(1)}, s32[8]{0:T(128)}, u32[]{:S(2)}) copy-start(s32[8]{0:T(128)} %param.14) | copy-start | bytes 100
  45.1 162.9 %all-to-all-start = ((bf16[4,2,24576]{2,1,0:T(2,128)(2,1)}), bf16[4,2,24576]{2,1,0:T(2,128)(2,1)S(1)}, u32[]{:S(2)}, u32[]{:S(2)}) async-start(bf16[4,2,24576]{2,1,0:T(2,128)(2,1)} %reshape.610), calls=%async_computation | async-start | bytes 786432 | tf_op jit(solution)/shard_map/all_to_all | solution.py:53
  157.3 41.2 %copy-start.10 = (s32[16,16]{1,0:T(8,128)S(1)}, s32[16,16]{1,0:T(8,128)}, u32[]{:S(2)}) copy-start(s32[16,16]{1,0:T(8,128)} %param.15) | copy-start | bytes 3076
  157.3 56.6 %copy-start.12 = (bf16[12,1,128]{2,0,1:T(8,128)(2,1)S(1)}, bf16[12,1,128]{2,0,1:T(8,128)(2,1)}, u32[]{:S(2)}) copy-start(bf16[12,1,128]{2,0,1:T(8,128)(2,1)} %param.12) | copy-start | bytes 9220
  191.8 30.6 %copy-start.13 = (bf16[12,1,128]{2,0,1:T(8,128)(2,1)S(1)}, bf16[12,1,128]{2,0,1:T(8,128)(2,1)}, u32[]{:S(2)}) copy-start(bf16[12,1,128]{2,0,1:T(8,128)(2,1)} %param.13) | copy-start | bytes 9220
  208.0 10.9 %all-to-all-start.1 = ((bf16[4,2,24576]{2,1,0:T(2,128)(2,1)}), bf16[4,2,24576]{2,1,0:T(2,128)(2,1)S(1)}, u32[]{:S(2)}, u32[]{:S(2)}) async-start(bf16[4,2,24576]{2,1,0:T(2,128)(2,1)} %reshape.612), calls=%async_computation.1 | async-start | bytes 786432 | tf_op jit(solution)/shard_map/all_to_all | solution.py:54
  218.9 16.3 %copy-start.3 = (bf16[4,2,24576]{2,1,0:T(2,128)(2,1)}, bf16[4,2,24576]{2,1,0:T(2,128)(2,1)S(1)}, u32[]{:S(2)}) copy-start(bf16[4,2,24576]{2,1,0:T(2,128)(2,1)S(1)} %all-to-all-done.1) | copy-start | bytes 1179652
  218.9 10.9 %all-to-all-start.3 = ((bf16[4,2,24576]{2,1,0:T(2,128)(2,1)}), bf16[4,2,24576]{2,1,0:T(2,128)(2,1)S(1)}, u32[]{:S(2)}, u32[]{:S(2)}) async-start(bf16[4,2,24576]{2,1,0:T(2,128)(2,1)} %reshape.616), calls=%async_computation.3 | async-start | bytes 786432 | tf_op jit(solution)/shard_map/all_to_all | solution.py:55
  229.8 5.4 %copy-start.4 = (bf16[4,2,24576]{2,1,0:T(2,128)(2,1)}, bf16[4,2,24576]{2,1,0:T(2,128)(2,1)S(1)}, u32[]{:S(2)}) copy-start(bf16[4,2,24576]{2,1,0:T(2,128)(2,1)S(1)} %all-to-all-done.3) | copy-start | bytes 1179652
  229.8 45.2 %all-to-all-start.2 = ((bf16[4,2,24576]{2,1,0:T(2,128)(2,1)}), bf16[4,2,24576]{2,1,0:T(2,128)(2,1)}, u32[]{:S(2)}, u32[]{:S(2)}) async-start(bf16[4,2,24576]{2,1,0:T(2,128)(2,1)} %reshape.614), calls=%async_computation.2 | async-start | bytes 786432 | tf_op jit(solution)/shard_map/all_to_all | solution.py:56
  247.8 42.7 %collective-permute-start.2 = (bf16[128,1536]{1,0:T(8,128)(2,1)}, bf16[128,1536]{1,0:T(8,128)(2,1)}, u32[]{:S(2)}, u32[]{:S(2)}) collective-permute-start(bf16[128,1536]{1,0:T(8,128)(2,1)} %bitcast.16), channel_id=1, source_target_pairs={{0,7},{1,0},{2,1},{3,2},{4,3},{5,4},{6,5},{7,6},{8,15},{9,8},{10,9... | collective-permute-start | bytes 1179656 | tf_op jit(solution)/shard_map/ppermute | solution.py:12
  253.0 43.9 %collective-permute-start = (bf16[128,1536]{1,0:T(8,128)(2,1)}, bf16[128,1536]{1,0:T(8,128)(2,1)}, u32[]{:S(2)}, u32[]{:S(2)}) collective-permute-start(bf16[128,1536]{1,0:T(8,128)(2,1)} %bitcast.16), channel_id=1, source_target_pairs={{0,1},{1,2},{2,3},{3,4},{4,5},{5,6},{6,7},{7,0},{8,9},{9,10},{10,1... | collective-permute-start | bytes 1179656 | tf_op jit(solution)/shard_map/ppermute | solution.py:12
  264.8 27.6 %collective-permute-start.3 = (bf16[128,1536]{1,0:T(8,128)(2,1)}, bf16[128,1536]{1,0:T(8,128)(2,1)}, u32[]{:S(2)}, u32[]{:S(2)}) collective-permute-start(bf16[128,1536]{1,0:T(8,128)(2,1)} %bitcast.18), channel_id=1, source_target_pairs={{0,7},{1,0},{2,1},{3,2},{4,3},{5,4},{6,5},{7,6},{8,15},{9,8},{10,9... | collective-permute-start | bytes 1179656 | tf_op jit(solution)/shard_map/ppermute | solution.py:12
  269.5 29.1 %collective-permute-start.1 = (bf16[128,1536]{1,0:T(8,128)(2,1)}, bf16[128,1536]{1,0:T(8,128)(2,1)}, u32[]{:S(2)}, u32[]{:S(2)}) collective-permute-start(bf16[128,1536]{1,0:T(8,128)(2,1)} %bitcast.18), channel_id=1, source_target_pairs={{0,1},{1,2},{2,3},{3,4},{4,5},{5,6},{6,7},{7,0},{8,9},{9,10},{10,1... | collective-permute-start | bytes 1179656 | tf_op jit(solution)/shard_map/ppermute | solution.py:12
  282.6 2.1 copy-start.2
  282.6 2.5 copy-start.9
  287.7 4.0 copy-start.8
  294.1 4.1 copy-start.7
  296.7 89.4 %collective-permute-start.9 = (bf16[128,1536]{0,1:T(8,128)(2,1)}, bf16[128,1536]{0,1:T(8,128)(2,1)}, u32[]{:S(2)}, u32[]{:S(2)}) collective-permute-start(bf16[128,1536]{0,1:T(8,128)(2,1)} %bitcast.49), channel_id=1, source_target_pairs={{0,1},{1,2},{2,3},{3,4},{4,5},{5,6},{6,7},{7,0},{8,9},{9,10},{10,1... | collective-permute-start | bytes 1179656 | tf_op jit(solution)/shard_map/ppermute | solution.py:12
  305.1 81.1 %collective-permute-start.8 = (bf16[128,1536]{0,1:T(8,128)(2,1)}, bf16[128,1536]{0,1:T(8,128)(2,1)}, u32[]{:S(2)}, u32[]{:S(2)}) collective-permute-start(bf16[128,1536]{0,1:T(8,128)(2,1)} %bitcast.213), channel_id=1, source_target_pairs={{0,7},{1,0},{2,1},{3,2},{4,3},{5,4},{6,5},{7,6},{8,15},{9,8},{10,9... | collective-permute-start | bytes 1179656 | tf_op jit(solution)/shard_map/ppermute | solution.py:12
  310.7 89.4 %collective-permute-start.13 = (bf16[128,1536]{1,0:T(8,128)(2,1)}, bf16[128,1536]{1,0:T(8,128)(2,1)}, u32[]{:S(2)}, u32[]{:S(2)}) collective-permute-start(bf16[128,1536]{1,0:T(8,128)(2,1)} %copy.322), channel_id=1, source_target_pairs={{0,1},{1,2},{2,3},{3,4},{4,5},{5,6},{6,7},{7,0},{8,9},{9,10},{10,1... | collective-permute-start | bytes 1179656 | tf_op jit(solution)/shard_map/ppermute | solution.py:12
  310.7 25.1 %collective-permute-start.6 = (bf16[128,1536]{1,0:T(8,128)(2,1)}, bf16[128,1536]{1,0:T(8,128)(2,1)S(1)}, u32[]{:S(2)}, u32[]{:S(2)}) collective-permute-start(bf16[128,1536]{1,0:T(8,128)(2,1)} %collective-permute-done.2), channel_id=1, source_target_pairs={{0,7},{1,0},{2,1},{3,2},{4,3},{5,4},{6,5},{7,6},{8,15},{9,8},{10,9... | collective-permute-start | bytes 1179656 | tf_op jit(solution)/shard_map/ppermute | solution.py:12
  317.9 18.2 %copy-start.6 = (pred[128,128]{1,0:T(8,128)(4,1)S(1)}, pred[128,128]{1,0:T(8,128)(4,1)}, u32[]{:S(2)}) copy-start(pred[128,128]{1,0:T(8,128)(4,1)} %get-tuple-element.27) | copy-start | bytes 49156
  317.9 34.7 %collective-permute-start.7 = (bf16[128,1536]{1,0:T(8,128)(2,1)}, bf16[128,1536]{1,0:T(8,128)(2,1)S(1)}, u32[]{:S(2)}, u32[]{:S(2)}) collective-permute-start(bf16[128,1536]{1,0:T(8,128)(2,1)} %collective-permute-done.3), channel_id=1, source_target_pairs={{0,7},{1,0},{2,1},{3,2},{4,3},{5,4},{6,5},{7,6},{8,15},{9,8},{10,9... | collective-permute-start | bytes 1179656 | tf_op jit(solution)/shard_map/ppermute | solution.py:12
  335.8 20.1 %collective-permute-start.4 = (bf16[128,1536]{1,0:T(8,128)(2,1)}, bf16[128,1536]{1,0:T(8,128)(2,1)S(1)}, u32[]{:S(2)}, u32[]{:S(2)}) collective-permute-start(bf16[128,1536]{1,0:T(8,128)(2,1)} %collective-permute-done), channel_id=1, source_target_pairs={{0,1},{1,2},{2,3},{3,4},{4,5},{5,6},{6,7},{7,0},{8,9},{9,10},{10,1... | collective-permute-start | bytes 1179656 | tf_op jit(solution)/shard_map/ppermute | solution.py:12
  352.6 15.1 %collective-permute-start.5 = (bf16[128,1536]{1,0:T(8,128)(2,1)}, bf16[128,1536]{1,0:T(8,128)(2,1)}, u32[]{:S(2)}, u32[]{:S(2)}) collective-permute-start(bf16[128,1536]{1,0:T(8,128)(2,1)} %collective-permute-done.1), channel_id=1, source_target_pairs={{0,1},{1,2},{2,3},{3,4},{4,5},{5,6},{6,7},{7,0},{8,9},{9,10},{10,1... | collective-permute-start | bytes 1179656 | tf_op jit(solution)/shard_map/ppermute | solution.py:12
  352.8 3.3 copy-start.5
  355.9 30.4 %collective-permute-start.11 = (bf16[128,1536]{0,1:T(8,128)(2,1)}, bf16[128,1536]{0,1:T(8,128)(2,1)}, u32[]{:S(2)}, u32[]{:S(2)}) collective-permute-start(bf16[128,1536]{0,1:T(8,128)(2,1)} %bitcast.53), channel_id=1, source_target_pairs={{0,2},{1,3},{2,4},{3,5},{4,6},{5,7},{6,0},{7,1},{8,10},{9,11},{10,... | collective-permute-start | bytes 1179656 | tf_op jit(solution)/shard_map/ppermute | solution.py:12
  370.7 19.6 %collective-permute-start.10 = (bf16[128,1536]{0,1:T(8,128)(2,1)}, bf16[128,1536]{0,1:T(8,128)(2,1)}, u32[]{:S(2)}, u32[]{:S(2)}) collective-permute-start(bf16[128,1536]{0,1:T(8,128)(2,1)} %bitcast.51), channel_id=1, source_target_pairs={{0,6},{1,7},{2,0},{3,1},{4,2},{5,3},{6,4},{7,5},{8,14},{9,15},{10,... | collective-permute-start | bytes 1179656 | tf_op jit(solution)/shard_map/ppermute | solution.py:12
  373.7 16.6 %copy-start.1 = (f32[128,12,128]{0,2,1:T(8,128)S(1)}, f32[128,12,128]{0,2,1:T(8,128)}, u32[]{:S(2)}) copy-start(f32[128,12,128]{0,2,1:T(8,128)} %copy.302) | copy-start | bytes 2359300
  377.8 18.9 %all-to-all-start.4 = ((bf16[4,2,24576]{2,1,0:T(2,128)(2,1)}), bf16[4,2,24576]{2,1,0:T(2,128)(2,1)S(1)}, u32[]{:S(2)}, u32[]{:S(2)}) async-start(bf16[4,2,24576]{2,1,0:T(2,128)(2,1)} %reshape.618), calls=%async_computation.4 | async-start | bytes 786432 | tf_op jit(solution)/shard_map/all_to_all | solution.py:114
  386.1 26.5 %copy-start = (f32[128,1536]{1,0:T(8,128)S(1)}, f32[128,1536]{1,0:T(8,128)}, u32[]{:S(2)}) copy-start(f32[128,1536]{1,0:T(8,128)} %copy.320) | copy-start | bytes 2359300
  386.1 14.0 %collective-permute-start.12 = (bf16[128,1536]{1,0:T(8,128)(2,1)}, bf16[128,1536]{1,0:T(8,128)(2,1)}, u32[]{:S(2)}, u32[]{:S(2)}) collective-permute-start(bf16[128,1536]{1,0:T(8,128)(2,1)} %copy.319), channel_id=1, source_target_pairs={{0,7},{1,0},{2,1},{3,2},{4,3},{5,4},{6,5},{7,6},{8,15},{9,8},{10,9... | collective-permute-start | bytes 1179656 | tf_op jit(solution)/shard_map/ppermute | solution.py:12
  386.2 18.7 %collective-permute-start.15 = (bf16[128,1536]{1,0:T(8,128)(2,1)}, bf16[128,1536]{1,0:T(8,128)(2,1)}, u32[]{:S(2)}, u32[]{:S(2)}) collective-permute-start(bf16[128,1536]{1,0:T(8,128)(2,1)} %copy.326), channel_id=1, source_target_pairs={{0,2},{1,3},{2,4},{3,5},{4,6},{5,7},{6,0},{7,1},{8,10},{9,11},{10,... | collective-permute-start | bytes 1179656 | tf_op jit(solution)/shard_map/ppermute | solution.py:12
  386.3 26.3 %collective-permute-start.14 = (bf16[128,1536]{1,0:T(8,128)(2,1)S(1)}, bf16[128,1536]{1,0:T(8,128)(2,1)}, u32[]{:S(2)}, u32[]{:S(2)}) collective-permute-start(bf16[128,1536]{1,0:T(8,128)(2,1)S(1)} %copy.324), channel_id=1, source_target_pairs={{0,6},{1,7},{2,0},{3,1},{4,2},{5,3},{6,4},{7,5},{8,14},{9,15},{10,... | collective-permute-start | bytes 1179656 | tf_op jit(solution)/shard_map/ppermute | solution.py:12
  396.7 22.2 %all-to-all-start.5 = ((bf16[4,2,24576]{2,1,0:T(2,128)(2,1)}), bf16[4,2,24576]{2,1,0:T(2,128)(2,1)S(1)}, u32[]{:S(2)}, u32[]{:S(2)}) async-start(bf16[4,2,24576]{2,1,0:T(2,128)(2,1)} %reshape.620), calls=%async_computation.5 | async-start | bytes 786432 | tf_op jit(solution)/shard_map/all_to_all | solution.py:115
  418.8 10.9 %all-to-all-start.6 = ((bf16[4,2,24576]{2,1,0:T(2,128)(2,1)}), bf16[4,2,24576]{2,1,0:T(2,128)(2,1)S(1)}, u32[]{:S(2)}, u32[]{:S(2)}) async-start(bf16[4,2,24576]{2,1,0:T(2,128)(2,1)} %reshape.622), calls=%async_computation.6 | async-start | bytes 786432 | tf_op jit(solution)/shard_map/all_to_all | solution.py:116
where the time goes:
time: 440 us; the launch traced here: 431 us
  other arithmetic  164 us (37%)
  local copies, waits for them, and re-layouts  105 us (24%)
  waiting for transfers between devices  73.7 us (17%)
  starting transfers between devices  53.1 us (12%)
  between operations  18 us (4%)
  matrix products  17.7 us (4%)
    unnamed x7, other arithmetic  147 us
    ppermute x16, waiting for transfers between devices, from_behind(): return lax.ppermute(value, axis, pairs)  56.4 us
    unnamed x50, local copies, waits for them, and re-layouts  52.8 us
    ppermute x16, starting transfers between devices, from_behind(): return lax.ppermute(value, axis, pairs)  23.8 us
    select_n x5, other arithmetic, allowed_for(): upper = jnp.where(low_rows[None, :], upper_left, upper_right)  11.1 us
  transfers between devices with their start and end apart: 23, of which 8 were waited for; matrix products, arithmetic and copies ran while one was open for 55% of the time, Pallas kernels for 0%

commit v1 on v0

v1 whole, which is shorter than its diff:
```python
import functools

import jax
import jax.numpy as jnp
from jax import lax
from jax.experimental import pallas as pl
from jax.experimental.pallas import tpu as pltpu
from jax.sharding import PartitionSpec as P

HD = 128
LOG2E = 1.4426950408889634
BIG = 1e30
CHUNKS = 4
LANE_PAD = 16


def kernel(
    n_head,
    n_blk,
    mults,
    q_ref, k_ref, v_ref, g_ref, ld_ref, assign_ref, mask_ref,
    dq_out, dk_out, dv_out,
    qgkv, rqg, rld, bias, dq_acc, dkv_acc, fin, dq_send, dq_recv,
    in_send, in_recv, ld_send, ld_recv, f_send, f_recv, b_send, b_recv, o_send, o_recv,
):
    rows = q_ref.shape[1]
    width = q_ref.shape[2] // n_head
    total_rows = rows * n_head
    half = total_rows // 2
    heads = width // HD
    hc = heads // CHUNKS
    cw = hc * HD
    scaling = HD ** -0.5
    n_rel = len(mults)
    hi = lax.axis_index("head")
    me = lax.axis_index("blk")
    sign = 1 - 2 * lax.rem(me, 2)
    slots = [lax.rem(me + m * sign + 2 * n_blk, n_blk) for m in mults]
    landing = [i if m % 2 else mults.index(-m) for i, m in enumerate(mults)]
    partners = [lax.rem(hi + r, n_head) for r in range(1, n_head)]
    outs = (dq_out, dk_out, dv_out)

    barrier = pltpu.get_barrier_semaphore()
    for p in partners:
        pl.semaphore_signal(barrier, inc=1, device_id={"head": p}, device_id_type=pl.DeviceIdType.MESH)
    for s in slots:
        pl.semaphore_signal(barrier, inc=1, device_id={"blk": s}, device_id_type=pl.DeviceIdType.MESH)
    pl.semaphore_wait(barrier, n_head - 1 + n_rel)

    def remote(src, dst, send, recv, where):
        return pltpu.make_async_remote_copy(
            src_ref=src, dst_ref=dst, send_sem=send, recv_sem=recv,
            device_id=where, device_id_type=pl.DeviceIdType.MESH,
        )

    def chunk(c):
        return pl.ds(pl.multiple_of(c * cw, HD), cw)

    my_rows = pl.ds(pl.multiple_of(hi * rows, rows), rows)
    my_cols = pl.ds(pl.multiple_of(hi * width, HD), width)

    def in_copy(array, ref, r, c):
        p = partners[r]
        return remote(
            ref.at[0, :, pl.ds(pl.multiple_of(p * width + c * cw, HD), cw)],
            qgkv.at[array, my_rows, chunk(c)],
            in_send.at[array, r, c], in_recv.at[array, r, c], {"head": p},
        )

    def ld_copy(i):
        return remote(ld_ref, rld.at[landing[i]], ld_send.at[i], ld_recv.at[landing[i]], {"blk": slots[i]})

    def ld_wait(i):
        remote(ld_ref, rld.at[i], ld_send.at[i], ld_recv.at[i], {"blk": slots[i]}).wait_recv()

    def f_copy(i, c, a):
        if mults[i] == -1:
            return remote(rqg.at[1, a, :, chunk(c)], rqg.at[3, a, :, chunk(c)],
                          f_send.at[i, a, c], f_recv.at[i, a, c], {"blk": slots[0]})
        j = landing[i]
        return remote(qgkv.at[a, :, chunk(c)], rqg.at[j, a, :, chunk(c)],
                      f_send.at[i, a, c], f_recv.at[j, a, c], {"blk": slots[i]})

    def f_wait(i, c):
        for a in range(2):
            remote(qgkv.at[a, :, chunk(c)], rqg.at[i, a, :, chunk(c)],
                   f_send.at[i, a, c], f_recv.at[i, a, c], {"blk": slots[i]}).wait_recv()

    def b_copy(i, c):
        if mults[i] == -1:
            j, where = 3, slots[0]
        else:
            j, where = landing[i], slots[i]
        return remote(dq_send.at[i, :, chunk(c)], dq_recv.at[j, :, chunk(c)],
                      b_send.at[i, c], b_recv.at[j, c], {"blk": where})

    def b_wait(i, c):
        remote(dq_send.at[i, :, chunk(c)], dq_recv.at[i, :, chunk(c)],
               b_send.at[i, c], b_recv.at[i, c], {"blk": slots[i]}).wait_recv()

    def o_copy(array, r, c):
        p = partners[r]
        return remote(
            fin.at[array, pl.ds(pl.multiple_of(p * rows, rows), rows), chunk(c)],
            outs[array].at[0, :, pl.ds(pl.multiple_of(hi * width + c * cw, HD), cw)],
            o_send.at[array, r, c], o_recv.at[array, r, c], {"head": p},
        )

    for arrays in ((0, 1), (2, 3)):
        for c in range(CHUNKS):
            for array in arrays:
                for r in range(n_head - 1):
                    in_copy(array, (q_ref, g_ref, k_ref, v_ref)[array], r, c).start()
    for i in range(n_rel):
        ld_copy(i).start()
    for array, ref in enumerate((q_ref, g_ref, k_ref, v_ref)):
        qgkv[array, my_rows, :] = ref[0, :, my_cols]

    key_ids = lax.broadcasted_iota(jnp.int32, (total_rows, total_rows), 0)
    query_ids = lax.broadcasted_iota(jnp.int32, (total_rows, total_rows), 1)
    key_low, query_low = key_ids < half, query_ids < half
    later = lax.rem(query_ids, half) >= lax.rem(key_ids, half)
    k_first = assign_ref[me]
    k_second = 2 * n_blk - 1 - k_first
    for i, s in enumerate([me] + slots):
        q_first = assign_ref[s]
        q_second = 2 * n_blk - 1 - q_first
        table = jnp.where(
            query_low,
            jnp.where(key_low, mask_ref[q_first, k_first], mask_ref[q_first, k_second]),
            jnp.where(key_low, mask_ref[q_second, k_first], mask_ref[q_second, k_second]),
        )
        allowed = (table == 1) | ((table == 2) & later)
        bias[i] = jnp.where(allowed, 0.0, -BIG)

    @pl.loop(0, CHUNKS)
    def _(c):
        for array in range(2):
            for r in range(n_head - 1):
                in_copy(array, (q_ref, g_ref)[array], r, c).wait_recv()
        for i, m in enumerate(mults):
            if m != -1:
                for a in range(2):
                    f_copy(i, c, a).start()

    for i in range(n_rel):
        ld_wait(i)

    def pair(which, c, q_of, g_of, ld_of, first, emit):
        for h in range(hc):
            head = c * hc + h
            cols = pl.ds(pl.multiple_of(head * HD, HD), HD)
            q, g, k, v = q_of(cols), g_of(cols), qgkv[2, :, cols], qgkv[3, :, cols]
            lse = ld_of[pl.ds(head, 1), :] * LOG2E
            delta = ld_of[pl.ds(LANE_PAD + head, 1), :]
            contract = (((1,), (1,)), ((), ()))
            s = lax.dot_general(k, q, contract, preferred_element_type=jnp.float32)
            p = jnp.exp2(s * (scaling * LOG2E) - lse + bias[which])
            dp = lax.dot_general(v, g, contract, preferred_element_type=jnp.float32)
            ds = (p * (dp - delta)).astype(jnp.bfloat16)
            dv = jnp.dot(p.astype(jnp.bfloat16), g, preferred_element_type=jnp.float32)
            dk = jnp.dot(ds, q, preferred_element_type=jnp.float32)
            dq = lax.dot_general(ds, k, (((0,), (0,)), ((), ())), preferred_element_type=jnp.float32)
            if first:
                dkv_acc[0, :, cols] = dk
                dkv_acc[1, :, cols] = dv
            else:
                dkv_acc[0, :, cols] += dk
                dkv_acc[1, :, cols] += dv
            emit(cols, dq * scaling)

    def own(c):
        def emit(cols, dq):
            dq_acc[:, cols] = dq
        pair(0, c, lambda x: qgkv[0, :, x], lambda x: qgkv[1, :, x], ld_ref, True, emit)

    def other(i, c):
        def emit(cols, dq):
            dq_send[i, :, cols] = dq.astype(jnp.bfloat16)
        pair(i + 1, c, lambda x: rqg[i, 0, :, x], lambda x: rqg[i, 1, :, x], rld.at[i], False, emit)

    def finish(array, c, value):
        fin[array, :, chunk(c)] = value.astype(jnp.bfloat16)
        for r in range(n_head - 1):
            o_copy(array, r, c).start()
        outs[array][0, :, pl.ds(pl.multiple_of(hi * width + c * cw, HD), cw)] = fin[array, my_rows, chunk(c)]

    direct = [i for i, m in enumerate(mults) if m != -1]

    @pl.loop(0, CHUNKS + 3)
    def _(step):
        @pl.when(step < CHUNKS)
        def _():
            c = step
            for array in (2, 3):
                for r in range(n_head - 1):
                    in_copy(array, (q_ref, g_ref, k_ref, v_ref)[array], r, c).wait_recv()
            own(c)
            f_wait(1, c)
            for a in range(2):
                f_copy(3, c, a).start()
            for i in direct:
                if i != 1:
                    f_wait(i, c)
                    other(i, c)
                    b_copy(i, c).start()
            other(1, c)

        @pl.when((step >= 1) & (step < CHUNKS + 1))
        def _():
            c = step - 1
            f_wait(3, c)
            other(3, c)
            b_copy(3, c).start()
            finish(1, c, dkv_acc[0, :, chunk(c)] * scaling)
            finish(2, c, dkv_acc[1, :, chunk(c)])

        @pl.when((step >= 2) & (step < CHUNKS + 2))
        def _():
            c = step - 2
            b_wait(3, c)
            both = dq_send[1, :, chunk(c)].astype(jnp.float32) + dq_recv[3, :, chunk(c)].astype(jnp.float32)
            dq_send[1, :, chunk(c)] = both.astype(jnp.bfloat16)
            b_copy(1, c).start()

        @pl.when(step >= 3)
        def _():
            c = step - 3
            total = dq_acc[:, chunk(c)]
            for i in direct:
                b_wait(i, c)
                total = total + dq_recv[i, :, chunk(c)].astype(jnp.float32)
            finish(0, c, total)

    for i in range(n_rel):
        ld_copy(i).wait_send()

    @pl.loop(0, CHUNKS)
    def _(c):
        for array in range(4):
            for r in range(n_head - 1):
                in_copy(array, (q_ref, g_ref, k_ref, v_ref)[array], r, c).wait_send()
        for i in range(n_rel):
            for a in range(2):
                f_copy(i, c, a).wait_send()
            b_copy(i, c).wait_send()
        for array in range(3):
            for r in range(n_head - 1):
                o_copy(array, r, c).wait_send()
                o_copy(array, r, c).wait_recv()


def local(queries, keys, values, out_grad, log_sum_exp, row_delta, assignment, block_mask):
    n_head, n_blk = lax.axis_size("head"), lax.axis_size("blk")
    cycle = min(4, n_blk // 4)
    mults = [1, 2, -2, -1] + [m * f for m in range(3, cycle + 1) for f in (1, -1)]
    n_rel = len(mults)
    rows, width = queries.shape[1], queries.shape[2] // n_head
    total = rows * n_head
    heads = log_sum_exp.shape[0]
    pad = ((0, LANE_PAD - heads), (0, 0))
    ld = jnp.concatenate([
        jnp.pad(log_sum_exp[:, 0, :].astype(jnp.float32), pad),
        jnp.pad(row_delta[:, 0, :].astype(jnp.float32), pad),
    ])
    vmem = pl.BlockSpec(memory_space=pltpu.VMEM)
    smem = pl.BlockSpec(memory_space=pltpu.SMEM)
    dma = pltpu.SemaphoreType.DMA
    out = jax.ShapeDtypeStruct(queries.shape, jnp.bfloat16)
    bf, f32 = jnp.bfloat16, jnp.float32
    return pl.pallas_call(
        functools.partial(kernel, n_head, n_blk, mults),
        out_shape=(out, out, out),
        in_specs=[vmem] * 5 + [smem] * 2,
        out_specs=(vmem, vmem, vmem),
        scratch_shapes=[
            pltpu.VMEM((4, total, width), bf),
            pltpu.VMEM((n_rel, 2, total, width), bf),
            pltpu.VMEM((n_rel,) + ld.shape, f32),
            pltpu.VMEM((n_rel + 1, total, total), f32),
            pltpu.VMEM((total, width), f32),
            pltpu.VMEM((2, total, width), f32),
            pltpu.VMEM((3, total, width), bf),
            pltpu.VMEM((n_rel, total, width), bf),
            pltpu.VMEM((n_rel, total, width), bf),
            dma((4, n_head - 1, CHUNKS)), dma((4, n_head - 1, CHUNKS)),
            dma((n_rel,)), dma((n_rel,)),
            dma((n_rel, 2, CHUNKS)), dma((n_rel, 2, CHUNKS)),
            dma((n_rel, CHUNKS)), dma((n_rel, CHUNKS)),
            dma((3, n_head - 1, CHUNKS)), dma((3, n_head - 1, CHUNKS)),
        ],
        compiler_params=pltpu.CompilerParams(
            collective_id=0, has_side_effects=True, vmem_limit_bytes=48 * 1024 * 1024
        ),
    )(queries, keys, values, out_grad, ld, assignment, block_mask)


def solution(mesh):
    token = P("blk", "head", None)
    stat = P("head", "blk", None)
    return jax.shard_map(
        local,
        mesh=mesh,
        in_specs=(token, token, token, token, stat, stat, P(), P()),
        out_specs=(token, token, token),
        check_vma=False,
    )
```

time: 440 us -> 81.1 us (0.18); the launches traced: 431 us -> 80.8 us
  other arithmetic: 164 us -> 0.72 us
  local copies, waits for them, and re-layouts: 105 us -> 6.22 us
  waiting for transfers between devices: 73.7 us -> 0 us
  Pallas kernels: 0 us -> 73.2 us
  starting transfers between devices: 53.1 us -> 0 us
  matrix products: 17.7 us -> 0 us
  between operations: 18 us -> 0.67 us
    unnamed x7 -> x0, other arithmetic: 147 us -> none
    pallas_call x0 -> x1, Pallas kernels: none -> 73.2 us  [local(): pl.pallas_call(functools.partial(kernel, n_head, n_blk, mults), out_shape...]
    ppermute x16 -> x0, waiting for transfers between devices: 56.4 us -> none  [from_behind(): return lax.ppermute(value, axis, pairs)]
    unnamed x50 -> x15, local copies, waits for them, and re-layouts: 52.8 us -> 6.22 us
    all_to_all x7 -> x0, starting transfers between devices: 29.3 us -> none  [the longest x1 6.92 us: local(): lax.all_to_all(query_grad, 'head', split_axis=1, concat_axis=2, tiled=True)]
    all_to_all x15 -> x0, local copies, waits for them, and re-layouts: 25.5 us -> none  [the longest x3 6.84 us: local(): lax.all_to_all(keys, 'head', split_axis=2, concat_axis=1, tiled=True)]
    ppermute x16 -> x0, starting transfers between devices: 23.8 us -> none  [from_behind(): return lax.ppermute(value, axis, pairs)]
    dot_general x25 -> x0, matrix products: 17.7 us -> none  [the longest x5 7.15 us: pair_terms(): jnp.einsum('hqk,khd->qhd', dscores, k_three, preferred_element_type=jnp.f...]
  transfers between devices with their start and end apart: 23 -> 0, of which waited for: 8 -> 0; matrix products, arithmetic and copies ran while one was open for 55% -> 0% of each run, Pallas kernels for 0% -> 0%
where the time goes in v1:
time: 81.1 us; the launch traced here: 80.8 us
  Pallas kernels  73.2 us (90%)
  local copies, waits for them, and re-layouts  6.22 us (8%)
    pallas_call x1, Pallas kernels, local(): pl.pallas_call(functools.partial(kernel, n_head, n_blk, mults), out_shape...  73.2 us
    unnamed x15, local copies, waits for them, and re-layouts  6.22 us

profile of v1, /device:TPU:0, one launch (start us, length us, event | category | flops | bytes accessed | tf_op | source)
XLA Modules:
  0.0 80.8 jit_solution(11426620765134325499)
XLA Ops:
  0.6 0.0 copy-start.4
  0.6 0.0 copy-start.5
  0.7 0.7 fusion.3.ld_ref
  1.4 0.0 copy-done.4
  1.4 0.0 copy-done.5
  1.4 0.0 copy-start
  1.4 1.0 %copy-done = bf16[1,32,6144]{2,1,0:T(8,128)(2,1)S(1)} copy-done((bf16[1,32,6144]{2,1,0:T(8,128)(2,1)S(1)}, bf16[1,32,6144]{2,1,0:T(8,128)(2,1)}, u32[]{:S(2)}) %copy-start) | copy-done | bytes 393240
  2.4 0.0 copy-start.1
  2.4 1.0 %copy-done.1 = bf16[1,32,6144]{2,1,0:T(8,128)(2,1)S(1)} copy-done((bf16[1,32,6144]{2,1,0:T(8,128)(2,1)S(1)}, bf16[1,32,6144]{2,1,0:T(8,128)(2,1)}, u32[]{:S(2)}) %copy-start.1) | copy-done | bytes 393240
  3.4 0.0 copy-start.2
  3.4 1.0 %copy-done.2 = bf16[1,32,6144]{2,1,0:T(8,128)(2,1)S(1)} copy-done((bf16[1,32,6144]{2,1,0:T(8,128)(2,1)S(1)}, bf16[1,32,6144]{2,1,0:T(8,128)(2,1)}, u32[]{:S(2)}) %copy-start.2) | copy-done | bytes 393240
  4.4 0.0 copy-start.3
  4.4 1.0 %copy-done.3 = bf16[1,32,6144]{2,1,0:T(8,128)(2,1)S(1)} copy-done((bf16[1,32,6144]{2,1,0:T(8,128)(2,1)S(1)}, bf16[1,32,6144]{2,1,0:T(8,128)(2,1)}, u32[]{:S(2)}) %copy-start.3) | copy-done | bytes 393240
  5.4 73.2 %shard_map.103 = (bf16[1,32,6144]{2,1,0:T(8,128)(2,1)S(1)}, bf16[1,32,6144]{2,1,0:T(8,128)(2,1)S(1)}, bf16[1,32,6144]{2,1,0:T(8,128)(2,1)S(1)}) custom-call(bf16[1,32,6144]{2,1,0:T(8,128)(2,1)S(1)} %copy-done, bf16[1,32,6144]{2,1,0:T(8,128)(2,1)S(1)} %copy-done.1, bf16[1,32,6144]{2,1,0:T(8,128)(2,1)S(1)} %copy-done.2, bf16[1,32,6144]{2,1,0:T(8,128)(2,1)S(1)} %copy-done.3, ...), custom_call_target="tpu_custom_call" | custom-call | tf_op jit(solution)/shard_map/pallas_call | solution.py:271
  78.6 0.7 copy.14
  79.3 0.7 copy.15
  80.1 0.7 copy.16
Async XLA Ops:
  0.6 0.7 copy-start.4
  0.6 0.7 copy-start.5
  1.4 1.0 %copy-start = (bf16[1,32,6144]{2,1,0:T(8,128)(2,1)S(1)}, bf16[1,32,6144]{2,1,0:T(8,128)(2,1)}, u32[]{:S(2)}) copy-start(bf16[1,32,6144]{2,1,0:T(8,128)(2,1)} %q_ref.1) | copy-start | bytes 1179652
  2.4 1.0 %copy-start.1 = (bf16[1,32,6144]{2,1,0:T(8,128)(2,1)S(1)}, bf16[1,32,6144]{2,1,0:T(8,128)(2,1)}, u32[]{:S(2)}) copy-start(bf16[1,32,6144]{2,1,0:T(8,128)(2,1)} %k_ref.1) | copy-start | bytes 1179652
  3.4 1.0 %copy-start.2 = (bf16[1,32,6144]{2,1,0:T(8,128)(2,1)S(1)}, bf16[1,32,6144]{2,1,0:T(8,128)(2,1)}, u32[]{:S(2)}) copy-start(bf16[1,32,6144]{2,1,0:T(8,128)(2,1)} %v_ref.1) | copy-start | bytes 1179652
  4.4 1.0 %copy-start.3 = (bf16[1,32,6144]{2,1,0:T(8,128)(2,1)S(1)}, bf16[1,32,6144]{2,1,0:T(8,128)(2,1)}, u32[]{:S(2)}) copy-start(bf16[1,32,6144]{2,1,0:T(8,128)(2,1)} %g_ref.1) | copy-start | bytes 1179652

commit v2 on v1

--- a/solution.py
+++ b/solution.py
@@ -11,6 +11,11 @@
 LOG2E = 1.4426950408889634
 BIG = 1e30
 CHUNKS = 4
+KV_PIECES = 2
+FIRST = "i0 i1 i2 i3"
+SECOND = "n0 n1 n2 n3 k0 k1"
+THIRD = "f0 g0 f1 g1 f2 g2 f3 g3"
+STEPS = ('h0', 'h1', 'h2', 'h3')
 LANE_PAD = 16
 
 
@@ -18,10 +23,10 @@
     n_head,
     n_blk,
     mults,
-    q_ref, k_ref, v_ref, g_ref, ld_ref, assign_ref, mask_ref,
+    q_ref, k_ref, v_ref, g_ref, lse_hbm, delta_hbm, assign_hbm, mask_hbm,
     dq_out, dk_out, dv_out,
-    qgkv, rqg, rld, bias, dq_acc, dkv_acc, fin, dq_send, dq_recv,
-    in_send, in_recv, ld_send, ld_recv, f_send, f_recv, b_send, b_recv, o_send, o_recv,
+    qgkv, rqg, ld_ref, rld, bias, dq_acc, dkv_acc, fin, dq_send, dq_recv, stats, assign_ref, mask_ref,
+    load, in_send, in_recv, kv_send, kv_recv, ld_send, ld_recv, f_send, f_recv, b_send, b_recv, o_send, o_recv,
 ):
     rows = q_ref.shape[1]
     width = q_ref.shape[2] // n_head
@@ -37,8 +42,26 @@
     sign = 1 - 2 * lax.rem(me, 2)
     slots = [lax.rem(me + m * sign + 2 * n_blk, n_blk) for m in mults]
     landing = [i if m % 2 else mults.index(-m) for i, m in enumerate(mults)]
-    partners = [lax.rem(hi + r, n_head) for r in range(1, n_head)]
+    sibling = hi + 1 - 2 * lax.rem(hi, 2)
+    partners = [sibling, lax.rem(hi + 2, n_head), lax.rem(sibling + 2, n_head)]
     outs = (dq_out, dk_out, dv_out)
+    ins = (q_ref, g_ref, k_ref, v_ref)
+    my_rows = pl.ds(pl.multiple_of(hi * rows, rows), rows)
+    my_cols = pl.ds(pl.multiple_of(hi * width, HD), width)
+    near = hi // 2
+    chip_rows = [pl.ds(pl.multiple_of(x * 2 * rows, 2 * rows), 2 * rows) for x in (near, 1 - near)]
+
+    loads = [
+        pltpu.make_async_copy(lse_hbm, stats.at[0], load.at[0]),
+        pltpu.make_async_copy(delta_hbm, stats.at[1], load.at[1]),
+        pltpu.make_async_copy(assign_hbm, assign_ref, load.at[2]),
+        pltpu.make_async_copy(mask_hbm, mask_ref, load.at[3]),
+    ] + [
+        pltpu.make_async_copy(ref.at[0, :, my_cols], qgkv.at[array, my_rows, :], load.at[4 + array])
+        for array, ref in enumerate(ins)
+    ]
+    for copy in loads:
+        copy.start()
 
     barrier = pltpu.get_barrier_semaphore()
     for p in partners:
@@ -56,35 +79,42 @@
     def chunk(c):
         return pl.ds(pl.multiple_of(c * cw, HD), cw)
 
-    my_rows = pl.ds(pl.multiple_of(hi * rows, rows), rows)
-    my_cols = pl.ds(pl.multiple_of(hi * width, HD), width)
-
-    def in_copy(array, ref, r, c):
+    def in_copy(array, r, c):
         p = partners[r]
         return remote(
-            ref.at[0, :, pl.ds(pl.multiple_of(p * width + c * cw, HD), cw)],
+            ins[array].at[0, :, pl.ds(pl.multiple_of(p * width + c * cw, HD), cw)],
             qgkv.at[array, my_rows, chunk(c)],
             in_send.at[array, r, c], in_recv.at[array, r, c], {"head": p},
         )
 
+    def kv_copy(array, r, piece):
+        p = partners[r]
+        kw = width // KV_PIECES
+        return remote(
+            ins[array].at[0, :, pl.ds(pl.multiple_of(p * width + piece * kw, HD), kw)],
+            qgkv.at[array, my_rows, pl.ds(pl.multiple_of(piece * kw, HD), kw)],
+            kv_send.at[array - 2, r, piece], kv_recv.at[array - 2, r, piece], {"head": p},
+        )
+
     def ld_copy(i):
         return remote(ld_ref, rld.at[landing[i]], ld_send.at[i], ld_recv.at[landing[i]], {"blk": slots[i]})
 
     def ld_wait(i):
         remote(ld_ref, rld.at[i], ld_send.at[i], ld_recv.at[i], {"blk": slots[i]}).wait_recv()
 
-    def f_copy(i, c, a):
+    def f_copy(i, c, part):
+        rs = chip_rows[part]
         if mults[i] == -1:
-            return remote(rqg.at[1, a, :, chunk(c)], rqg.at[3, a, :, chunk(c)],
-                          f_send.at[i, a, c], f_recv.at[i, a, c], {"blk": slots[0]})
+            return remote(rqg.at[1, :, rs, chunk(c)], rqg.at[3, :, rs, chunk(c)],
+                          f_send.at[i, part, c], f_recv.at[i, part, c], {"blk": slots[0]})
         j = landing[i]
-        return remote(qgkv.at[a, :, chunk(c)], rqg.at[j, a, :, chunk(c)],
-                      f_send.at[i, a, c], f_recv.at[j, a, c], {"blk": slots[i]})
-
-    def f_wait(i, c):
-        for a in range(2):
-            remote(qgkv.at[a, :, chunk(c)], rqg.at[i, a, :, chunk(c)],
-                   f_send.at[i, a, c], f_recv.at[i, a, c], {"blk": slots[i]}).wait_recv()
+        return remote(qgkv.at[pl.ds(0, 2), rs, chunk(c)], rqg.at[j, :, rs, chunk(c)],
+                      f_send.at[i, part, c], f_recv.at[j, part, c], {"blk": slots[i]})
+
+    def f_wait(i, c, part):
+        rs = chip_rows[part]
+        remote(qgkv.at[pl.ds(0, 2), rs, chunk(c)], rqg.at[i, :, rs, chunk(c)],
+               f_send.at[i, part, c], f_recv.at[i, part, c], {"blk": slots[i]}).wait_recv()
 
     def b_copy(i, c):
         if mults[i] == -1:
@@ -106,15 +136,55 @@
             o_send.at[array, r, c], o_recv.at[array, r, c], {"head": p},
         )
 
-    for arrays in ((0, 1), (2, 3)):
-        for c in range(CHUNKS):
-            for array in arrays:
-                for r in range(n_head - 1):
-                    in_copy(array, (q_ref, g_ref, k_ref, v_ref)[array], r, c).start()
+    direct = [i for i, m in enumerate(mults) if m != -1]
+    order = [2, 1] + [i for i in direct if i not in (1, 2)]
+
+    def send_part(c, part):
+        for r in ((0,), (1, 2))[part]:
+            for array in range(2):
+                in_copy(array, r, c).wait_recv()
+        for i in order:
+            f_copy(i, c, part).start()
+
+    def forward(c, part):
+        f_wait(1, c, part)
+        f_copy(3, c, part).start()
+
+    def start_in(c):
+        for r in range(n_head - 1):
+            for array in range(2):
+                in_copy(array, r, c).start()
+
+    def start_kv(piece):
+        for r in range(n_head - 1):
+            for array in (2, 3):
+                kv_copy(array, r, piece).start()
+
+    per = CHUNKS // KV_PIECES
+    actions = {
+        "i": start_in,
+        "n": lambda c: send_part(c, 0),
+        "f": lambda c: send_part(c, 1),
+        "g": lambda c: forward(c, 0),
+        "h": lambda c: forward(c, 1),
+        "k": start_kv,
+    }
+
+    def act(plan):
+        for word in plan.split():
+            actions[word[0]](int(word[1:]))
+
+    act(FIRST)
+    for copy in loads[4:6]:
+        copy.wait()
+    act(SECOND)
+
+    for copy in loads[:4]:
+        copy.wait()
+    for part in range(2):
+        ld_ref[pl.ds(part * LANE_PAD, heads), :] = stats[part].astype(jnp.float32)
     for i in range(n_rel):
         ld_copy(i).start()
-    for array, ref in enumerate((q_ref, g_ref, k_ref, v_ref)):
-        qgkv[array, my_rows, :] = ref[0, :, my_cols]
 
     key_ids = lax.broadcasted_iota(jnp.int32, (total_rows, total_rows), 0)
     query_ids = lax.broadcasted_iota(jnp.int32, (total_rows, total_rows), 1)
@@ -133,16 +203,9 @@
         allowed = (table == 1) | ((table == 2) & later)
         bias[i] = jnp.where(allowed, 0.0, -BIG)
 
-    @pl.loop(0, CHUNKS)
-    def _(c):
-        for array in range(2):
-            for r in range(n_head - 1):
-                in_copy(array, (q_ref, g_ref)[array], r, c).wait_recv()
-        for i, m in enumerate(mults):
-            if m != -1:
-                for a in range(2):
-                    f_copy(i, c, a).start()
-
+    for copy in loads[6:]:
+        copy.wait()
+    act(THIRD)
     for i in range(n_rel):
         ld_wait(i)
 
@@ -185,23 +248,27 @@
             o_copy(array, r, c).start()
         outs[array][0, :, pl.ds(pl.multiple_of(hi * width + c * cw, HD), cw)] = fin[array, my_rows, chunk(c)]
 
-    direct = [i for i, m in enumerate(mults) if m != -1]
-
     @pl.loop(0, CHUNKS + 3)
     def _(step):
         @pl.when(step < CHUNKS)
         def _():
             c = step
-            for array in (2, 3):
-                for r in range(n_head - 1):
-                    in_copy(array, (q_ref, g_ref, k_ref, v_ref)[array], r, c).wait_recv()
+            for later_c in range(CHUNKS):
+                @pl.when(c == later_c)
+                def _():
+                    act(STEPS[later_c])
+
+            for piece in range(KV_PIECES):
+                @pl.when(c == piece * per)
+                def _():
+                    for array in (2, 3):
+                        for r in range(n_head - 1):
+                            kv_copy(array, r, piece).wait_recv()
             own(c)
-            f_wait(1, c)
-            for a in range(2):
-                f_copy(3, c, a).start()
             for i in direct:
                 if i != 1:
-                    f_wait(i, c)
+                    f_wait(i, c, 0)
+                    f_wait(i, c, 1)
                     other(i, c)
                     b_copy(i, c).start()
             other(1, c)
@@ -209,7 +276,8 @@
         @pl.when((step >= 1) & (step < CHUNKS + 1))
         def _():
             c = step - 1
-            f_wait(3, c)
+            f_wait(3, c, 0)
+            f_wait(3, c, 1)
             other(3, c)
             b_copy(3, c).start()
             finish(1, c, dkv_acc[0, :, chunk(c)] * scaling)
@@ -235,11 +303,16 @@
     for i in range(n_rel):
         ld_copy(i).wait_send()
 
+    for piece in range(KV_PIECES):
+        for r in range(n_head - 1):
+            for array in (2, 3):
+                kv_copy(array, r, piece).wait_send()
+
     @pl.loop(0, CHUNKS)
     def _(c):
-        for array in range(4):
+        for array in range(2):
             for r in range(n_head - 1):
-                in_copy(array, (q_ref, g_ref, k_ref, v_ref)[array], r, c).wait_send()
+                in_copy(array, r, c).wait_send()
         for i in range(n_rel):
             for a in range(2):
                 f_copy(i, c, a).wait_send()
@@ -257,42 +330,42 @@
     n_rel = len(mults)
     rows, width = queries.shape[1], queries.shape[2] // n_head
     total = rows * n_head
-    heads = log_sum_exp.shape[0]
-    pad = ((0, LANE_PAD - heads), (0, 0))
-    ld = jnp.concatenate([
-        jnp.pad(log_sum_exp[:, 0, :].astype(jnp.float32), pad),
-        jnp.pad(row_delta[:, 0, :].astype(jnp.float32), pad),
-    ])
     vmem = pl.BlockSpec(memory_space=pltpu.VMEM)
-    smem = pl.BlockSpec(memory_space=pltpu.SMEM)
+    hbm = pl.BlockSpec(memory_space=pl.ANY)
     dma = pltpu.SemaphoreType.DMA
     out = jax.ShapeDtypeStruct(queries.shape, jnp.bfloat16)
     bf, f32 = jnp.bfloat16, jnp.float32
     return pl.pallas_call(
         functools.partial(kernel, n_head, n_blk, mults),
         out_shape=(out, out, out),
-        in_specs=[vmem] * 5 + [smem] * 2,
+        in_specs=[hbm] * 8,
         out_specs=(vmem, vmem, vmem),
         scratch_shapes=[
             pltpu.VMEM((4, total, width), bf),
             pltpu.VMEM((n_rel, 2, total, width), bf),
-            pltpu.VMEM((n_rel,) + ld.shape, f32),
+            pltpu.VMEM((2 * LANE_PAD, total), f32),
+            pltpu.VMEM((n_rel, 2 * LANE_PAD, total), f32),
             pltpu.VMEM((n_rel + 1, total, total), f32),
             pltpu.VMEM((total, width), f32),
             pltpu.VMEM((2, total, width), f32),
             pltpu.VMEM((3, total, width), bf),
             pltpu.VMEM((n_rel, total, width), bf),
             pltpu.VMEM((n_rel, total, width), bf),
-            dma((4, n_head - 1, CHUNKS)), dma((4, n_head - 1, CHUNKS)),
+            pltpu.VMEM((2, log_sum_exp.shape[0], total), bf),
+            pltpu.SMEM(assignment.shape, jnp.int32),
+            pltpu.SMEM(block_mask.shape, jnp.int32),
+            dma((8,)),
+            dma((2, n_head - 1, CHUNKS)), dma((2, n_head - 1, CHUNKS)),
+            dma((2, n_head - 1, KV_PIECES)), dma((2, n_head - 1, KV_PIECES)),
             dma((n_rel,)), dma((n_rel,)),
             dma((n_rel, 2, CHUNKS)), dma((n_rel, 2, CHUNKS)),
             dma((n_rel, CHUNKS)), dma((n_rel, CHUNKS)),
             dma((3, n_head - 1, CHUNKS)), dma((3, n_head - 1, CHUNKS)),
         ],
         compiler_params=pltpu.CompilerParams(
-            collective_id=0, has_side_effects=True, vmem_limit_bytes=48 * 1024 * 1024
+            collective_id=0, has_side_effects=True, vmem_limit_bytes=60 * 1024 * 1024
         ),
-    )(queries, keys, values, out_grad, ld, assignment, block_mask)
+    )(queries, keys, values, out_grad, log_sum_exp[:, 0], row_delta[:, 0], assignment, block_mask)
 
 
 def solution(mesh):

time: 81.1 us -> 74.8 us (0.922)
  Pallas kernels: 73.2 us -> 70.3 us
  local copies, waits for them, and re-layouts: 6.22 us -> 3.7 us
    pallas_call x1, Pallas kernels: 73.2 us -> 70.3 us  [local(): pl.pallas_call(functools.partial(kernel, n_head, n_blk, mults), out_shape...]
    unnamed x15 -> x7, local copies, waits for them, and re-layouts: 6.22 us -> 3.7 us
where the time goes in v2:
time: 74.8 us; the launch traced here: 74.7 us
  Pallas kernels  70.3 us (94%)
  local copies, waits for them, and re-layouts  3.7 us (5%)
    pallas_call x1, Pallas kernels, local(): pl.pallas_call(functools.partial(kernel, n_head, n_blk, mults), out_shape...  70.3 us
    unnamed x7, local copies, waits for them, and re-layouts  3.7 us

profile of v2, /device:TPU:0, one launch (start us, length us, event | category | flops | bytes accessed | tf_op | source)
XLA Modules:
  0.0 74.7 jit_solution(3125623533365152906)
XLA Ops:
  0.6 70.3 %shard_map.103 = (bf16[1,32,6144]{2,1,0:T(8,128)(2,1)}, bf16[1,32,6144]{2,1,0:T(8,128)(2,1)}, bf16[1,32,6144]{2,1,0:T(8,128)(2,1)}) custom-call(bf16[1,32,6144]{2,1,0:T(8,128)(2,1)} %q_ref.1, bf16[1,32,6144]{2,1,0:T(8,128)(2,1)} %k_ref.1, bf16[1,32,6144]{2,1,0:T(8,128)(2,1)} %v_ref.1, bf16[1,32,6144]{2,1,0:T(8,128)(2,1)} %g_ref.1, bf16[12,128]{1,0:T(8,128)(2,1)} %bitcast.2, ...), custom_call_target="tpu_custom_call" | custom-call | tf_op jit(solution)/shard_map/pallas_call | solution.py:338
  70.9 0.0 copy-start.1
  71.0 1.8 %copy.14 = bf16[1,32,6144]{2,1,0:T(8,128)(2,1)} copy(bf16[1,32,6144]{2,1,0:T(8,128)(2,1)} %get-tuple-element.6) | data formatting | bytes 786432
  72.8 0.0 copy-done.1
  72.8 0.0 copy-start
  72.8 0.7 copy.15
  73.5 0.4 copy-done
  73.9 0.7 copy.16
Async XLA Ops:
  70.9 1.8 %copy-start.1 = (bf16[1,32,6144]{2,1,0:T(8,128)(2,1)S(1)}, bf16[1,32,6144]{2,1,0:T(8,128)(2,1)}, u32[]{:S(2)}) copy-start(bf16[1,32,6144]{2,1,0:T(8,128)(2,1)} %get-tuple-element.7) | copy-start | bytes 1179652
  72.8 1.1 %copy-start = (bf16[1,32,6144]{2,1,0:T(8,128)(2,1)S(1)}, bf16[1,32,6144]{2,1,0:T(8,128)(2,1)}, u32[]{:S(2)}) copy-start(bf16[1,32,6144]{2,1,0:T(8,128)(2,1)} %get-tuple-element.8) | copy-start | bytes 1179652

commit v3 on v2

--- a/solution.py
+++ b/solution.py
@@ -12,10 +12,10 @@
 BIG = 1e30
 CHUNKS = 4
 KV_PIECES = 2
-FIRST = "i0 i1 i2 i3"
-SECOND = "n0 n1 n2 n3 k0 k1"
-THIRD = "f0 g0 f1 g1 f2 g2 f3 g3"
-STEPS = ('h0', 'h1', 'h2', 'h3')
+FIRST = "i"
+SECOND = "nk"
+THIRD = ("f", "g")
+STEP = "h"
 LANE_PAD = 16
 
 
@@ -171,8 +171,9 @@
     }
 
     def act(plan):
-        for word in plan.split():
-            actions[word[0]](int(word[1:]))
+        for name in plan:
+            for c in range(KV_PIECES if name == "k" else CHUNKS):
+                actions[name](c)
 
     act(FIRST)
     for copy in loads[4:6]:
@@ -205,7 +206,10 @@
 
     for copy in loads[6:]:
         copy.wait()
-    act(THIRD)
+    for group in THIRD:
+        for c in range(CHUNKS):
+            for name in group:
+                actions[name](c)
     for i in range(n_rel):
         ld_wait(i)
 
@@ -253,10 +257,8 @@
         @pl.when(step < CHUNKS)
         def _():
             c = step
-            for later_c in range(CHUNKS):
-                @pl.when(c == later_c)
-                def _():
-                    act(STEPS[later_c])
+            for name in STEP:
+                actions[name](c)
 
             for piece in range(KV_PIECES):
                 @pl.when(c == piece * per)

time: 74.8 us -> 74.8 us (level)
  no operation moved by 1% of the time
where the time goes in v3:
time: 74.8 us; the launch traced here: 74.7 us
  Pallas kernels  70.3 us (94%)
  local copies, waits for them, and re-layouts  3.7 us (5%)
    pallas_call x1, Pallas kernels, local(): pl.pallas_call(functools.partial(kernel, n_head, n_blk, mults), out_shape...  70.3 us
    unnamed x7, local copies, waits for them, and re-layouts  3.7 us

profile of v3, /device:TPU:0, one launch (start us, length us, event | category | flops | bytes accessed | tf_op | source)
XLA Modules:
  0.0 74.7 jit_solution(1913355707857405533)
XLA Ops:
  0.6 70.3 %shard_map.103 = (bf16[1,32,6144]{2,1,0:T(8,128)(2,1)}, bf16[1,32,6144]{2,1,0:T(8,128)(2,1)}, bf16[1,32,6144]{2,1,0:T(8,128)(2,1)}) custom-call(bf16[1,32,6144]{2,1,0:T(8,128)(2,1)} %q_ref.1, bf16[1,32,6144]{2,1,0:T(8,128)(2,1)} %k_ref.1, bf16[1,32,6144]{2,1,0:T(8,128)(2,1)} %v_ref.1, bf16[1,32,6144]{2,1,0:T(8,128)(2,1)} %g_ref.1, bf16[12,128]{1,0:T(8,128)(2,1)} %bitcast.2, ...), custom_call_target="tpu_custom_call" | custom-call | tf_op jit(solution)/shard_map/pallas_call | solution.py:340
  70.9 0.0 copy-start.1
  71.0 1.8 %copy.14 = bf16[1,32,6144]{2,1,0:T(8,128)(2,1)} copy(bf16[1,32,6144]{2,1,0:T(8,128)(2,1)} %get-tuple-element.6) | data formatting | bytes 786432
  72.8 0.0 copy-done.1
  72.8 0.0 copy-start
  72.8 0.7 copy.15
  73.5 0.4 copy-done
  73.9 0.7 copy.16
Async XLA Ops:
  70.9 1.8 %copy-start.1 = (bf16[1,32,6144]{2,1,0:T(8,128)(2,1)S(1)}, bf16[1,32,6144]{2,1,0:T(8,128)(2,1)}, u32[]{:S(2)}) copy-start(bf16[1,32,6144]{2,1,0:T(8,128)(2,1)} %get-tuple-element.7) | copy-start | bytes 1179652
  72.8 1.1 %copy-start = (bf16[1,32,6144]{2,1,0:T(8,128)(2,1)S(1)}, bf16[1,32,6144]{2,1,0:T(8,128)(2,1)}, u32[]{:S(2)}) copy-start(bf16[1,32,6144]{2,1,0:T(8,128)(2,1)} %get-tuple-element.8) | copy-start | bytes 1179652
